TPU v7x, 512 devices: a whole 4x4x16 slice. The times are simulated.
512 devices in a mesh: dp: 16 (over y, x), tp: 32 (over z, core).
Axes of the slice: x: 4, y: 4, z: 16, core: 2. Of those that a mesh axis runs over, the one named last changes fastest.
Arguments:
- token_codes: bfloat16 [8192, 3584], P(('dp', 'tp')), parts along dimension 0, may hold values from -127 to 127
- token_scales: bfloat16 [8192], P(('dp', 'tp')), parts along dimension 0, may hold values from 0.0049743652 to 0.049804688
- live_counts: int32 [512], P(('dp', 'tp')), parts along dimension 0, may hold values from 0 to 16, as said below
- gate_codes: bfloat16 [3584, 9216], P(None, 'tp'), may hold values from -127 to 127
- up_codes: bfloat16 [3584, 9216], P(None, 'tp'), may hold values from -127 to 127
- gate_scales: float32 [9216], P('tp'), may hold values from 2e-05 to 0.0018
- up_scales: float32 [9216], P('tp'), may hold values from 2e-05 to 0.0018
Outputs:
- down_input: bfloat16 [8192, 9216], P('dp', 'tp'), parts along dimension 0
- row_peak: float32 [8192], P('dp'), parts along dimension 0
There are 16 independent parts, one for each index of `dp`. A program takes and returns all parts, laid end to end along the dimension named above; an argument that names none is the same for every part. Nothing has to cross between parts.
Inputs may be any that keep to these rules, and one draw needn't show every extreme that they name: `live_counts`: the counts of one group sum to exactly 256, and some device of every group holds 16.
All inputs are finite; a program needn't handle non-finite values. Where the computation divides by a largest or mean magnitude, that divisor is 1e-20 or more.
Results may differ from a plain program's by a relative error of at most 0.014.
Values may be sent and summed in bfloat16 or wider, within the bound.
A program may use at most 64 MiB of HBM per device.

v0:
```python
import jax
import jax.numpy as jnp
from jax import lax
from jax.sharding import PartitionSpec as P


def project_rows(row_codes, row_scales, gate_codes, up_codes, gate_scales, up_scales):
    scale_col = row_scales.astype(jnp.float32)[:, None]
    gate_acc = jnp.dot(row_codes, gate_codes, preferred_element_type=jnp.float32)
    up_acc = jnp.dot(row_codes, up_codes, preferred_element_type=jnp.float32)
    gate_value = gate_acc * scale_col * gate_scales[None, :]
    up_value = up_acc * scale_col * up_scales[None, :]
    return (jax.nn.silu(gate_value) * up_value).astype(jnp.bfloat16)


def shards(token_codes, token_scales, live_counts, gate_codes, up_codes, gate_scales, up_scales):
    slot_count = token_codes.shape[0]
    slot_range = jnp.arange(slot_count, dtype=jnp.int32)
    slot_alive = slot_range < live_counts[0]
    sent_codes = jnp.where(slot_alive[:, None], token_codes, jnp.zeros_like(token_codes))
    sent_scales = jnp.where(slot_alive, token_scales, jnp.zeros_like(token_scales))
    all_codes, all_scales = (
        lax.all_gather(sent_codes, "tp", axis=0, tiled=True),
        lax.all_gather(sent_scales, "tp", axis=0, tiled=True),
    )
    hidden = project_rows(all_codes, all_scales, gate_codes, up_codes, gate_scales, up_scales)
    wide = hidden.astype(jnp.float32)
    local_peak = jnp.max(jnp.abs(wide), axis=1)
    row_peak = jnp.maximum(lax.pmax(local_peak, "tp"), 1e-05)
    down_input = (wide / row_peak[:, None]).astype(jnp.bfloat16)
    return (down_input, row_peak)


def solution(mesh):
    in_specs = (
        P(("dp", "tp"), None),
        P(("dp", "tp")),
        P(("dp", "tp")),
        P(None, "tp"),
        P(None, "tp"),
        P("tp"),
        P("tp"),
    )
    out_specs = (P("dp", "tp"), P("dp"))
    return jax.shard_map(shards, mesh=mesh, in_specs=in_specs, out_specs=out_specs, check_vma=False)
```

profile of v0, /device:TPU:1, one launch (start us, length us, event | category | flops | bytes accessed | tf_op | source)
XLA Modules:
  0.0 148.5 jit_solution(8786435663120344036)
XLA Ops:
  7.2 0.0 copy-start
  7.2 0.0 all-gather.2.cloned.1.call-start
  8.0 1.6 %broadcast_select_fusion = bf16[16,3584]{1,0:T(8,128)(2,1)} fusion(bf16[16,3584]{1,0:T(8,128)(2,1)} %param.7, pred[16]{0:T(512)(128)(4,1)S(1)} %iota_compare_fusion), kind=kLoop, calls=%fused_computation.9 | loop fusion | flops 57344 | bytes 229392 | tf_op jit(solution)/shard_map/jit(_where)/select_n | solution.py:20
  9.6 0.0 all-gather.2.cloned.1.call-update
  9.7 1.3 dynamic-slice
  11.5 0.7 broadcast_select_fusion.1
  12.2 0.2 dynamic-update-slice
  12.4 54.7 %all-reduce = bf16[512]{0:T(512)(128)(2,1)S(1)} all-reduce(bf16[512]{0:T(512)(128)(2,1)S(1)} %dynamic-update-slice), channel_id=1, replica_groups=mesh['dp'=16,'tp'=32] {'tp'}, use_global_device_ids=true, to_apply=%add | all-reduce | flops 512 | bytes 2048
  67.1 0.0 copy-start.3
  67.1 22.9 %all-gather.2.cloned.1.call-done = bf16[512,3584]{1,0:T(8,128)(2,1)} async-done(((bf16[16,3584]{1,0:T(8,128)(2,1)}), bf16[512,3584]{1,0:T(8,128)(2,1)}) %all-gather.2.cloned.1.call-update) | async-done | bytes 3670032 | tf_op jit(solution)/shard_map/all_gather | solution.py:23
  90.1 0.0 copy-start.2
  90.1 4.1 %fusion = f32[512,288]{0,1:T(8,128)S(1)} fusion(bf16[512,3584]{1,0:T(8,128)(2,1)} %all-gather.2.cloned.1.call-done, bf16[3584,288]{0,1:T(8,128)(2,1)} %param.10, f32[288]{0:T(512)} %param.12, f32[512]{0:T(512)S(1)} %convert_element_type.12), kind=kOutput, calls=%fused_computation.2 | convolution fusion | flops 1057259520 | bytes 6327424 | tf_op jit(solution)/shard_map/dot_general | solution.py:9
  94.1 0.0 copy-done
  94.2 0.0 copy-done.3
  94.2 0.0 copy-done.2
  94.2 1.3 abs_reduce_fusion
  95.5 45.4 %pmax.7 = f32[512]{0:T(512)S(1)} all-reduce(f32[512]{0:T(512)S(1)} %get-tuple-element.2), channel_id=1, replica_groups=mesh['dp'=16,'tp'=32] {'tp'}, use_global_device_ids=true, to_apply=%region_1.2 | all-reduce | flops 512 | bytes 4096 | tf_op jit(solution)/shard_map/pmax | solution.py:29
  140.9 0.0 copy-start.1
  140.9 0.8 divide_convert_fusion
  141.7 0.0 copy-done.1
  (4 shorter events, 0.0 us)
Async XLA Ops:
  7.2 87.0 %copy-start = (bf16[3584,288]{0,1:T(8,128)(2,1)S(1)}, bf16[3584,288]{0,1:T(8,128)(2,1)}, u32[]{:S(2)}) copy-start(bf16[3584,288]{0,1:T(8,128)(2,1)} %param.11) | copy-start | bytes 6193156
  7.2 82.9 %all-gather.2.cloned.1.call-start = ((), (), s32[]{:S(2)}) async-start(), calls=%async_computation | async-start | bytes 3784704 | tf_op jit(solution)/shard_map/all_gather | solution.py:23
  67.1 27.0 %copy-start.3 = (f32[288]{0:T(512)S(1)}, f32[288]{0:T(512)}, u32[]{:S(2)}) copy-start(f32[288]{0:T(512)} %param.13) | copy-start | bytes 3460
  90.1 4.1 %copy-start.2 = (bf16[512,3584]{1,0:T(8,128)(2,1)S(1)}, bf16[512,3584]{1,0:T(8,128)(2,1)}, u32[]{:S(2)}) copy-start(bf16[512,3584]{1,0:T(8,128)(2,1)} %all-gather.2.cloned.1.call-done) | copy-start | bytes 11010052
  140.9 0.8 copy-start.1
Sparse Core Ops, SparseCore 0:
  10.7 79.3 all-gather.1
where the time goes:
time: 150 us; the launch traced here: 149 us
  blocking collectives  100 us (67%)
  waiting for transfers between devices  22.9 us (15%)
  between operations  15.4 us (10%)
  matrix products  5.39 us (4%)
  other arithmetic  3.07 us (2%)
  local copies, waits for them, and re-layouts  1.51 us (1%)
    unnamed x1, blocking collectives  54.7 us
    pmax x1, blocking collectives, shards(): row_peak = jnp.maximum(lax.pmax(local_peak, 'tp'), 1e-05)  45.4 us
    all_gather x1, waiting for transfers between devices, shards(): lax.all_gather(sent_codes, 'tp', axis=0, tiled=True)  22.9 us
    dot_general x1, matrix products, project_rows(): jnp.dot(row_codes, gate_codes, preferred_element_type=jnp.float32)  4.06 us
  transfers between devices with their start and end apart: 1, of which 1 were waited for; matrix products, arithmetic and copies ran while one was open for 1% of the time, Pallas kernels for 0%

commit v1 on v0

v1 whole, which is shorter than its diff:
```python
import functools

import jax
import jax.numpy as jnp
from jax import lax
from jax.experimental import pallas as pl
from jax.experimental.pallas import tpu as pltpu
from jax.sharding import PartitionSpec as P

MESH = pl.DeviceIdType.MESH
SLOTS = 16
PIECES = 4
LANES = 128


def kernel(
    tp, width, hidden_units,
    codes_hbm, scales_ref, counts_ref, gate_hbm, up_hbm, gate_scales_ref, up_scales_ref,
    hidden_ref, peaks_ref,
    rows_buf, gate_buf, up_buf, local_peaks, own_peaks, all_peaks,
    send_sem, recv_sem, sib_send, sib_recv, peak_send, peak_recv, load_sem,
):
    me = lax.axis_index("tp")
    chips = tp // 2
    far = chips // 2
    sibling = me + 1 - 2 * lax.rem(me, 2)
    chip = me // 2
    row_count = tp * SLOTS
    full = width + LANES

    def at(distance):
        return lax.rem(me + 2 * distance + 2 * tp, tp)

    def rows_of(device):
        return pl.ds(pl.multiple_of(device * SLOTS, SLOTS), SLOTS)

    def chip_rows(distance):
        start = lax.rem(chip + distance + chips, chips) * (2 * SLOTS)
        return pl.ds(pl.multiple_of(start, 2 * SLOTS), 2 * SLOTS)

    tiles = full // LANES
    edges = [(tiles * s) // PIECES * LANES for s in range(PIECES + 1)]
    piece = [pl.ds(a, b - a) for a, b in zip(edges[:-1], edges[1:])]
    signs = (1, -1)

    barrier = pltpu.get_barrier_semaphore()
    for device in (at(1), at(-1), sibling):
        pl.semaphore_signal(barrier, inc=1, device_id={"tp": device}, device_id_type=MESH)
    own_copy = pltpu.make_async_copy(codes_hbm, rows_buf.at[rows_of(me), pl.ds(0, width)], load_sem.at[0])
    own_copy.start()
    gate_copy = pltpu.make_async_copy(gate_hbm, gate_buf, load_sem.at[1])
    gate_copy.start()
    up_copy = pltpu.make_async_copy(up_hbm, up_buf, load_sem.at[2])
    up_copy.start()
    row_id = lax.broadcasted_iota(jnp.int32, (SLOTS, SLOTS), 0)
    col_id = lax.broadcasted_iota(jnp.int32, (SLOTS, SLOTS), 1)
    kept = (row_id == col_id) & (row_id < counts_ref[0])
    spread = jnp.where(kept, scales_ref[...].astype(jnp.float32), 0.0)
    scale_col = jnp.sum(spread, axis=1, keepdims=True)
    rows_buf[rows_of(me), pl.ds(width, LANES)] = jnp.broadcast_to(scale_col, (SLOTS, LANES)).astype(jnp.bfloat16)
    own_copy.wait()
    pl.semaphore_wait(barrier, 3)

    def active(way, hop, s):
        return hop < far or (s < PIECES // 2) == (way == 0)

    def ring(way, hop, s, block):
        return pltpu.make_async_remote_copy(
            src_ref=rows_buf.at[rows_of(block), piece[s]],
            dst_ref=rows_buf.at[rows_of(block), piece[s]],
            send_sem=send_sem.at[way, hop - 1, s],
            recv_sem=recv_sem.at[way, hop - 1, s],
            device_id={"tp": at(signs[way])},
            device_id_type=MESH,
        )

    def share(way, hop, s, block):
        return pltpu.make_async_remote_copy(
            src_ref=rows_buf.at[rows_of(block), piece[s]],
            dst_ref=rows_buf.at[rows_of(block), piece[s]],
            send_sem=sib_send.at[way, hop, s],
            recv_sem=sib_recv.at[way, hop, s],
            device_id={"tp": sibling},
            device_id_type=MESH,
        )

    def project(distances):
        x = jnp.concatenate([rows_buf[chip_rows(d), pl.ds(0, width)] for d in distances], axis=0)
        scale = jnp.concatenate([rows_buf[chip_rows(d), pl.ds(width, LANES)] for d in distances], axis=0)
        scale = scale[:, 0:1].astype(jnp.float32)
        gate = jnp.dot(x, gate_buf[...], preferred_element_type=jnp.float32) * scale * gate_scales_ref[...]
        up = jnp.dot(x, up_buf[...], preferred_element_type=jnp.float32) * scale * up_scales_ref[...]
        hidden = (gate / (1.0 + jnp.exp(-gate)) * up).astype(jnp.bfloat16)
        peak = jnp.max(jnp.abs(hidden.astype(jnp.float32)), axis=1, keepdims=True)
        peak = jnp.broadcast_to(peak, (peak.shape[0], LANES))
        for i, d in enumerate(distances):
            part = slice(i * 2 * SLOTS, (i + 1) * 2 * SLOTS)
            hidden_ref[chip_rows(d), :] = hidden[part]
            local_peaks[chip_rows(d), :] = peak[part]

    def wait_shared(hop):
        for s in range(PIECES):
            for way in (0, 1):
                if active(way, hop, s) and not (hop == 0 and way == 1):
                    share(way, hop, s, me).wait_recv()

    for s in range(PIECES):
        for way in (0, 1):
            ring(way, 1, s, me).start()
    for s in range(PIECES):
        share(0, 0, s, me).start()
    for hop in range(1, far + 1):
        for s in range(PIECES):
            for way in (0, 1):
                if not active(way, hop, s):
                    continue
                block = at(-signs[way] * hop)
                ring(way, hop, s, block).wait_recv()
                if hop < far and active(way, hop + 1, s):
                    ring(way, hop + 1, s, block).start()
                share(way, hop, s, block).start()
        if hop == 2:
            gate_copy.wait()
            up_copy.wait()
            wait_shared(0)
            wait_shared(1)
            project((0, 1, -1))
        elif hop in (4, 6):
            wait_shared(hop - 2)
            wait_shared(hop - 1)
            project((hop - 2, 2 - hop, hop - 1, 1 - hop))
        elif hop == 7:
            wait_shared(6)
            project((6, -6))
    wait_shared(7)
    wait_shared(8)
    project((7, -7, 8))

    diagonal = lax.broadcasted_iota(jnp.int32, (LANES, LANES), 0) == lax.broadcasted_iota(jnp.int32, (LANES, LANES), 1)
    groups = row_count // LANES
    for g in range(groups):
        picked = jnp.where(diagonal, local_peaks[g * LANES:(g + 1) * LANES, :], 0.0)
        own_peaks[g:g + 1, :] = jnp.max(picked, axis=0, keepdims=True)

    def peak_copy(step):
        return pltpu.make_async_remote_copy(
            src_ref=own_peaks,
            dst_ref=all_peaks.at[step - 1],
            send_sem=peak_send.at[step - 1],
            recv_sem=peak_recv.at[step - 1],
            device_id={"tp": lax.rem(me + step, tp)},
            device_id_type=MESH,
        )

    order = sorted(range(1, tp), key=lambda step: -min(step, tp - step))
    for step in order:
        peak_copy(step).start()
    for hop in range(1, far + 1):
        for s in range(PIECES):
            for way in (0, 1):
                if active(way, hop, s):
                    ring(way, hop, s, me).wait_send()
                    share(way, hop, s, me).wait_send()
    for s in range(PIECES):
        share(0, 0, s, me).wait_send()
    for step in reversed(order):
        peak_copy(step).wait()
    peaks = jnp.maximum(jnp.max(all_peaks[...], axis=0), own_peaks[...])
    peaks_ref[...] = jnp.maximum(peaks, 1e-5)


def shards(token_codes, token_scales, live_counts, gate_codes, up_codes, gate_scales, up_scales):
    tp = lax.axis_size("tp")
    width = token_codes.shape[1]
    hidden_units = gate_codes.shape[1]
    row_count = tp * SLOTS
    groups = row_count // LANES
    whole = pl.BlockSpec(memory_space=pltpu.VMEM)
    hbm = pl.BlockSpec(memory_space=pl.ANY)
    far = tp // 4
    dma = pltpu.SemaphoreType.DMA
    hidden, peaks = pl.pallas_call(
        functools.partial(kernel, tp, width, hidden_units),
        out_shape=(
            jax.ShapeDtypeStruct((row_count, hidden_units), jnp.bfloat16),
            jax.ShapeDtypeStruct((groups, LANES), jnp.float32),
        ),
        in_specs=[hbm, whole, pl.BlockSpec(memory_space=pltpu.SMEM), hbm, hbm, whole, whole],
        out_specs=(whole, whole),
        scratch_shapes=[
            pltpu.VMEM((row_count, width + LANES), jnp.bfloat16),
            pltpu.VMEM((width, hidden_units), jnp.bfloat16),
            pltpu.VMEM((width, hidden_units), jnp.bfloat16),
            pltpu.VMEM((row_count, LANES), jnp.float32),
            pltpu.VMEM((groups, LANES), jnp.float32),
            pltpu.VMEM((tp - 1, groups, LANES), jnp.float32),
            dma((2, far, PIECES)),
            dma((2, far, PIECES)),
            dma((2, far + 1, PIECES)),
            dma((2, far + 1, PIECES)),
            dma((tp - 1,)),
            dma((tp - 1,)),
            dma((3,)),
        ],
        compiler_params=pltpu.CompilerParams(
            collective_id=0, has_side_effects=True, vmem_limit_bytes=40 << 20
        ),
    )(
        token_codes, token_scales[None, :], live_counts, gate_codes, up_codes,
        gate_scales[None, :], up_scales[None, :],
    )
    row_peak = peaks.reshape(row_count)
    down_input = (hidden.astype(jnp.float32) / row_peak[:, None]).astype(jnp.bfloat16)
    return (down_input, row_peak)


def solution(mesh):
    in_specs = (
        P(("dp", "tp"), None),
        P(("dp", "tp")),
        P(("dp", "tp")),
        P(None, "tp"),
        P(None, "tp"),
        P("tp"),
        P("tp"),
    )
    out_specs = (P("dp", "tp"), P("dp"))
    return jax.shard_map(shards, mesh=mesh, in_specs=in_specs, out_specs=out_specs, check_vma=False)
```

time: 150 us -> 67.2 us (0.45)
  blocking collectives: 100 us -> 0 us
  Pallas kernels: 0 us -> 53.1 us
  waiting for transfers between devices: 22.9 us -> 0 us
  between operations: 15.4 us -> 1.32 us
  local copies, waits for them, and re-layouts: 1.51 us -> 12.3 us
  matrix products: 5.39 us -> 0 us
  other arithmetic: 3.07 us -> 0.15 us
    unnamed x1 -> x0, blocking collectives: 54.7 us -> none
    pallas_call x0 -> x1, Pallas kernels: none -> 53.1 us  [shards(): pl.pallas_call(functools.partial(kernel, tp, width, hidden_units), out_sh...]
    pmax x1 -> x0, blocking collectives: 45.4 us -> none  [shards(): row_peak = jnp.maximum(lax.pmax(local_peak, 'tp'), 1e-05)]
    all_gather x1 -> x0, waiting for transfers between devices: 22.9 us -> none  [shards(): lax.all_gather(sent_codes, 'tp', axis=0, tiled=True)]
    unnamed x11 -> x10, local copies, waits for them, and re-layouts: 1.51 us -> 10.9 us
    dot_general x2 -> x0, matrix products: 5.39 us -> none  [the longest x1 4.06 us: project_rows(): jnp.dot(row_codes, gate_codes, preferred_element_type=jnp.float32)]
    select_n x2 -> x0, other arithmetic: 2.29 us -> none  [the longest x1 1.63 us: shards(): jnp.where(slot_alive[:, None], token_codes, jnp.zeros_like(token_codes))]
  transfers between devices with their start and end apart: 1 -> 0, of which waited for: 1 -> 0; matrix products, arithmetic and copies ran while one was open for 1% -> 0% of each run, Pallas kernels for 0% -> 0%
where the time goes in v1:
time: 67.2 us; the launch traced here: 66.9 us
  Pallas kernels  53.1 us (79%)
  local copies, waits for them, and re-layouts  12.3 us (18%)
  between operations  1.32 us (2%)
    pallas_call x1, Pallas kernels, shards(): pl.pallas_call(functools.partial(kernel, tp, width, hidden_units), out_sh...  53.1 us
    unnamed x10, local copies, waits for them, and re-layouts  10.9 us

profile of v1, /device:TPU:1, one launch (start us, length us, event | category | flops | bytes accessed | tf_op | source)
XLA Modules:
  0.0 66.9 jit_solution(6560535552212901345)
XLA Ops:
  1.3 0.7 %broadcast_in_dim.10.gate_scales_ref = f32[1,288]{1,0:T(1,128)S(1)} reshape(f32[288]{0:T(512)} %param.12) | data formatting | bytes 2304 | tf_op jit(solution)/shard_map/broadcast_in_dim | solution.py:210
  2.0 0.7 %broadcast_in_dim.11.up_scales_ref = f32[1,288]{1,0:T(1,128)S(1)} reshape(f32[288]{0:T(512)} %param.13) | data formatting | bytes 2304 | tf_op jit(solution)/shard_map/broadcast_in_dim | solution.py:210
  2.6 3.2 %copy.9.gate_hbm = bf16[3584,288]{1,0:T(8,128)(2,1)S(1)} copy(bf16[3584,288]{0,1:T(8,128)(2,1)} %param.10) | data formatting | bytes 4128768 | tf_op args[3]
  5.9 0.0 copy-start.1
  5.9 0.0 copy-start.2
  5.9 4.4 %copy.10.up_hbm = bf16[3584,288]{1,0:T(8,128)(2,1)} copy(bf16[3584,288]{0,1:T(8,128)(2,1)} %param.11) | data formatting | bytes 4128768 | tf_op args[4]
  10.3 0.0 copy-done.1
  10.3 0.0 copy-done.2
  10.3 0.0 copy-start
  10.3 1.8 %copy-done = bf16[3584,288]{1,0:T(8,128)(2,1)S(1)} copy-done((bf16[3584,288]{1,0:T(8,128)(2,1)S(1)}, bf16[3584,288]{1,0:T(8,128)(2,1)}, u32[]{:S(2)}) %copy-start) | copy-done | bytes 2064408
  12.1 53.1 %shard_map.86 = (bf16[512,288]{1,0:T(8,128)(2,1)S(1)}, f32[4,128]{1,0:T(4,128)S(1)}) custom-call(bf16[16,3584]{1,0:T(8,128)(2,1)S(1)} %copy-done.1, bf16[1,16]{1,0:T(2,128)(2,1)S(1)} %bitcast.4, s32[1]{0:T(128)S(6)} %copy.13.counts_ref, bf16[3584,288]{1,0:T(8,128)(2,1)S(1)} %copy.9.gate_hbm, bf16[3584,288]{1,0:T(8,128)(2,1)S(1)} %copy-done, ...), custom_call_target="tpu_custom_call" | custom-call | tf_op jit(solution)/shard_map/pallas_call | solution.py:182
  65.2 0.2 divide_convert_fusion
  65.4 0.9 %copy.11 = bf16[512,288]{0,1:T(8,128)(2,1)} copy(bf16[512,288]{1,0:T(8,128)(2,1)S(1)} %divide_convert_fusion) | data formatting | bytes 589824
  66.3 0.6 copy.14
Async XLA Ops:
  5.9 4.4 %copy-start.1 = (bf16[16,3584]{1,0:T(8,128)(2,1)S(1)}, bf16[16,3584]{1,0:T(8,128)(2,1)}, u32[]{:S(2)}) copy-start(bf16[16,3584]{1,0:T(8,128)(2,1)} %codes_hbm.1) | copy-start | bytes 344068
  5.9 4.4 %copy-start.2 = (bf16[16]{0:T(256)(128)(2,1)S(1)}, bf16[16]{0:T(256)(128)(2,1)}, u32[]{:S(2)}) copy-start(bf16[16]{0:T(256)(128)(2,1)} %param.8) | copy-start | bytes 100
  10.3 1.8 %copy-start = (bf16[3584,288]{1,0:T(8,128)(2,1)S(1)}, bf16[3584,288]{1,0:T(8,128)(2,1)}, u32[]{:S(2)}) copy-start(bf16[3584,288]{1,0:T(8,128)(2,1)} %copy.10.up_hbm) | copy-start | bytes 6193156

commit v2 on v1

--- a/solution.py
+++ b/solution.py
@@ -13,11 +13,16 @@
 LANES = 128
 
 
+def equal_ids(rows, columns):
+    shape = (rows, columns)
+    return lax.broadcasted_iota(jnp.int32, shape, 0) == lax.broadcasted_iota(jnp.int32, shape, 1)
+
+
 def kernel(
-    tp, width, hidden_units,
+    tp, width, units,
     codes_hbm, scales_ref, counts_ref, gate_hbm, up_hbm, gate_scales_ref, up_scales_ref,
     hidden_ref, peaks_ref,
-    rows_buf, gate_buf, up_buf, local_peaks, own_peaks, all_peaks,
+    rows_buf, weights, channel_scales, own_peaks, all_peaks,
     send_sem, recv_sem, sib_send, sib_recv, peak_send, peak_recv, load_sem,
 ):
     me = lax.axis_index("tp")
@@ -25,7 +30,8 @@
     far = chips // 2
     sibling = me + 1 - 2 * lax.rem(me, 2)
     chip = me // 2
-    row_count = tp * SLOTS
+    groups = tp * SLOTS // LANES
+    group_chips = chips // groups
     full = width + LANES
 
     def at(distance):
@@ -33,10 +39,6 @@
 
     def rows_of(device):
         return pl.ds(pl.multiple_of(device * SLOTS, SLOTS), SLOTS)
-
-    def chip_rows(distance):
-        start = lax.rem(chip + distance + chips, chips) * (2 * SLOTS)
-        return pl.ds(pl.multiple_of(start, 2 * SLOTS), 2 * SLOTS)
 
     tiles = full // LANES
     edges = [(tiles * s) // PIECES * LANES for s in range(PIECES + 1)]
@@ -48,13 +50,11 @@
         pl.semaphore_signal(barrier, inc=1, device_id={"tp": device}, device_id_type=MESH)
     own_copy = pltpu.make_async_copy(codes_hbm, rows_buf.at[rows_of(me), pl.ds(0, width)], load_sem.at[0])
     own_copy.start()
-    gate_copy = pltpu.make_async_copy(gate_hbm, gate_buf, load_sem.at[1])
+    gate_copy = pltpu.make_async_copy(gate_hbm, weights.at[pl.ds(0, units)], load_sem.at[1])
     gate_copy.start()
-    up_copy = pltpu.make_async_copy(up_hbm, up_buf, load_sem.at[2])
+    up_copy = pltpu.make_async_copy(up_hbm, weights.at[pl.ds(units, units)], load_sem.at[2])
     up_copy.start()
-    row_id = lax.broadcasted_iota(jnp.int32, (SLOTS, SLOTS), 0)
-    col_id = lax.broadcasted_iota(jnp.int32, (SLOTS, SLOTS), 1)
-    kept = (row_id == col_id) & (row_id < counts_ref[0])
+    kept = equal_ids(SLOTS, SLOTS) & (lax.broadcasted_iota(jnp.int32, (SLOTS, SLOTS), 0) < counts_ref[0])
     spread = jnp.where(kept, scales_ref[...].astype(jnp.float32), 0.0)
     scale_col = jnp.sum(spread, axis=1, keepdims=True)
     rows_buf[rows_of(me), pl.ds(width, LANES)] = jnp.broadcast_to(scale_col, (SLOTS, LANES)).astype(jnp.bfloat16)
@@ -84,19 +84,26 @@
             device_id_type=MESH,
         )
 
-    def project(distances):
-        x = jnp.concatenate([rows_buf[chip_rows(d), pl.ds(0, width)] for d in distances], axis=0)
-        scale = jnp.concatenate([rows_buf[chip_rows(d), pl.ds(width, LANES)] for d in distances], axis=0)
-        scale = scale[:, 0:1].astype(jnp.float32)
-        gate = jnp.dot(x, gate_buf[...], preferred_element_type=jnp.float32) * scale * gate_scales_ref[...]
-        up = jnp.dot(x, up_buf[...], preferred_element_type=jnp.float32) * scale * up_scales_ref[...]
-        hidden = (gate / (1.0 + jnp.exp(-gate)) * up).astype(jnp.bfloat16)
-        peak = jnp.max(jnp.abs(hidden.astype(jnp.float32)), axis=1, keepdims=True)
-        peak = jnp.broadcast_to(peak, (peak.shape[0], LANES))
-        for i, d in enumerate(distances):
-            part = slice(i * 2 * SLOTS, (i + 1) * 2 * SLOTS)
-            hidden_ref[chip_rows(d), :] = hidden[part]
-            local_peaks[chip_rows(d), :] = peak[part]
+    first = chip // group_chips
+    nearer = 2 * (lax.rem(chip, group_chips) // (group_chips // 2)) - 1
+    ranked = [lax.rem(first + groups + step, groups) for step in (0, nearer, -nearer, 2)]
+
+    def project(picked):
+        spans = [pl.ds(pl.multiple_of(ranked[i] * LANES, LANES), LANES) for i in picked]
+        x = jnp.concatenate([rows_buf[span, pl.ds(0, width)] for span in spans], axis=0)
+        values = lax.dot_general(
+            weights[...], x, (((1,), (1,)), ((), ())), preferred_element_type=jnp.float32
+        )
+        for i, span in enumerate(spans):
+            spread = jnp.where(equal_ids(LANES, LANES), rows_buf[span, pl.ds(width, LANES)].astype(jnp.float32), 0.0)
+            scale = jnp.sum(spread, axis=0, keepdims=True)
+            part = values[:, i * LANES:(i + 1) * LANES]
+            gate = part[:units] * scale * channel_scales[:, 0:1]
+            up = part[units:] * scale * channel_scales[:, 1:2]
+            hidden = (gate / (1.0 + jnp.exp(-gate)) * up).astype(jnp.bfloat16)
+            hidden_ref[:, span] = hidden
+            peak = jnp.max(jnp.abs(hidden.astype(jnp.float32)), axis=0, keepdims=True)
+            own_peaks[pl.ds(ranked[picked[i]], 1), :] = peak
 
     def wait_shared(hop):
         for s in range(PIECES):
@@ -119,28 +126,19 @@
                 if hop < far and active(way, hop + 1, s):
                     ring(way, hop + 1, s, block).start()
                 share(way, hop, s, block).start()
-        if hop == 2:
+        if hop == 1:
+            for k, ref in enumerate((gate_scales_ref, up_scales_ref)):
+                spread = jnp.where(equal_ids(units, units), ref[...], 0.0)
+                channel_scales[:, k:k + 1] = jnp.sum(spread, axis=1, keepdims=True)
+        elif hop == 6:
             gate_copy.wait()
             up_copy.wait()
-            wait_shared(0)
-            wait_shared(1)
-            project((0, 1, -1))
-        elif hop in (4, 6):
-            wait_shared(hop - 2)
-            wait_shared(hop - 1)
-            project((hop - 2, 2 - hop, hop - 1, 1 - hop))
-        elif hop == 7:
-            wait_shared(6)
-            project((6, -6))
-    wait_shared(7)
-    wait_shared(8)
-    project((7, -7, 8))
-
-    diagonal = lax.broadcasted_iota(jnp.int32, (LANES, LANES), 0) == lax.broadcasted_iota(jnp.int32, (LANES, LANES), 1)
-    groups = row_count // LANES
-    for g in range(groups):
-        picked = jnp.where(diagonal, local_peaks[g * LANES:(g + 1) * LANES, :], 0.0)
-        own_peaks[g:g + 1, :] = jnp.max(picked, axis=0, keepdims=True)
+            for earlier in range(6):
+                wait_shared(earlier)
+            project((0, 1))
+    for earlier in (6, 7, 8):
+        wait_shared(earlier)
+    project((2, 3))
 
     def peak_copy(step):
         return pltpu.make_async_remote_copy(
@@ -172,26 +170,25 @@
 def shards(token_codes, token_scales, live_counts, gate_codes, up_codes, gate_scales, up_scales):
     tp = lax.axis_size("tp")
     width = token_codes.shape[1]
-    hidden_units = gate_codes.shape[1]
+    units = gate_codes.shape[1]
     row_count = tp * SLOTS
     groups = row_count // LANES
     whole = pl.BlockSpec(memory_space=pltpu.VMEM)
-    hbm = pl.BlockSpec(memory_space=pl.ANY)
+    hbm = pl.BlockSpec(memory_space=pltpu.HBM)
     far = tp // 4
     dma = pltpu.SemaphoreType.DMA
     hidden, peaks = pl.pallas_call(
-        functools.partial(kernel, tp, width, hidden_units),
+        functools.partial(kernel, tp, width, units),
         out_shape=(
-            jax.ShapeDtypeStruct((row_count, hidden_units), jnp.bfloat16),
+            jax.ShapeDtypeStruct((units, row_count), jnp.bfloat16),
             jax.ShapeDtypeStruct((groups, LANES), jnp.float32),
         ),
         in_specs=[hbm, whole, pl.BlockSpec(memory_space=pltpu.SMEM), hbm, hbm, whole, whole],
         out_specs=(whole, whole),
         scratch_shapes=[
             pltpu.VMEM((row_count, width + LANES), jnp.bfloat16),
-            pltpu.VMEM((width, hidden_units), jnp.bfloat16),
-            pltpu.VMEM((width, hidden_units), jnp.bfloat16),
-            pltpu.VMEM((row_count, LANES), jnp.float32),
+            pltpu.VMEM((2 * units, width), jnp.bfloat16),
+            pltpu.VMEM((units, LANES), jnp.float32),
             pltpu.VMEM((groups, LANES), jnp.float32),
             pltpu.VMEM((tp - 1, groups, LANES), jnp.float32),
             dma((2, far, PIECES)),
@@ -203,15 +200,15 @@
             dma((3,)),
         ],
         compiler_params=pltpu.CompilerParams(
-            collective_id=0, has_side_effects=True, vmem_limit_bytes=40 << 20
+            collective_id=0, has_side_effects=True, vmem_limit_bytes=60 << 20
         ),
     )(
-        token_codes, token_scales[None, :], live_counts, gate_codes, up_codes,
+        token_codes, token_scales[None, :], live_counts, gate_codes.T, up_codes.T,
         gate_scales[None, :], up_scales[None, :],
     )
     row_peak = peaks.reshape(row_count)
-    down_input = (hidden.astype(jnp.float32) / row_peak[:, None]).astype(jnp.bfloat16)
-    return (down_input, row_peak)
+    down_input = (hidden.astype(jnp.float32) / row_peak[None, :]).astype(jnp.bfloat16)
+    return (down_input.T, row_peak)
 
 
 def solution(mesh):

time: 67.2 us -> 61.4 us (0.914)
  local copies, waits for them, and re-layouts: 12.3 us -> 3.75 us
  other arithmetic: 0.15 us -> 1.73 us
  Pallas kernels: 53.1 us -> 54.4 us
    unnamed x10 -> x1, local copies, waits for them, and re-layouts: 10.9 us -> 1.26 us
    transpose x0 -> x1, other arithmetic: none -> 1.73 us  [shards(): return (down_input.T, row_peak)]
    pallas_call x1, Pallas kernels: 53.1 us -> 54.4 us  [shards(): pl.pallas_call(functools.partial(kernel, tp, width, units), out_shape=(ja...]
where the time goes in v2:
time: 61.4 us; the launch traced here: 61.2 us
  Pallas kernels  54.4 us (89%)
  local copies, waits for them, and re-layouts  3.75 us (6%)
  other arithmetic  1.73 us (3%)
  between operations  1.29 us (2%)
    pallas_call x1, Pallas kernels, shards(): pl.pallas_call(functools.partial(kernel, tp, width, units), out_shape=(ja...  54.4 us
    transpose x1, other arithmetic, shards(): return (down_input.T, row_peak)  1.73 us
    unnamed x1, local copies, waits for them, and re-layouts  1.26 us
    broadcast_in_dim x1, local copies, waits for them, and re-layouts, shards(): gate_scales[None, :]  1.25 us
    broadcast_in_dim x1, local copies, waits for them, and re-layouts, shards(): up_scales[None, :]  1.24 us

profile of v2, /device:TPU:1, one launch (start us, length us, event | category | flops | bytes accessed | tf_op | source)
XLA Modules:
  0.0 61.2 jit_solution(4438561416905860381)
XLA Ops:
  1.3 1.2 %broadcast_in_dim.10.gate_scales_ref = f32[1,288]{1,0:T(1,128)} reshape(f32[288]{0:T(512)} %param.12) | data formatting | bytes 2304 | tf_op jit(solution)/shard_map/broadcast_in_dim | solution.py:207
  2.5 1.2 %broadcast_in_dim.11.up_scales_ref = f32[1,288]{1,0:T(1,128)} reshape(f32[288]{0:T(512)} %param.13) | data formatting | bytes 2304 | tf_op jit(solution)/shard_map/broadcast_in_dim | solution.py:207
  3.8 54.4 %shard_map.86 = (bf16[288,512]{1,0:T(8,128)(2,1)}, f32[4,128]{1,0:T(4,128)}) custom-call(bf16[16,3584]{1,0:T(8,128)(2,1)} %codes_hbm.1, bf16[1,16]{1,0:T(2,128)(2,1)} %bitcast.10, s32[1]{0:T(128)S(6)} %copy.10.counts_ref, bf16[288,3584]{1,0:T(8,128)(2,1)} %bitcast.6, bf16[288,3584]{1,0:T(8,128)(2,1)} %bitcast.7, f32[1,288]{1,0:T(1,128)} %broadcast_in_dim.10.gate_scales_ref, ...), custom_call_target="tpu_custom_call" | custom-call | tf_op jit(solution)/shard_map/pallas_call | solution.py:180
  58.2 1.7 %fusion = bf16[512,288]{0,1:T(8,128)(2,1)} fusion(bf16[288,512]{1,0:T(8,128)(2,1)} %get-tuple-element.4, f32[512]{0:T(512)} %bitcast.8), kind=kLoop, calls=%fused_computation.1 | loop fusion | flops 442368 | bytes 591872 | tf_op jit(solution)/shard_map/transpose | solution.py:211
  59.9 1.3 %copy.11 = f32[512]{0:T(512)} copy(f32[512]{0:T(512)} %bitcast.9) | data formatting | bytes 4096

commit v3 on v2

--- a/solution.py
+++ b/solution.py
@@ -21,8 +21,8 @@
 def kernel(
     tp, width, units,
     codes_hbm, scales_ref, counts_ref, gate_hbm, up_hbm, gate_scales_ref, up_scales_ref,
-    hidden_ref, peaks_ref,
-    rows_buf, weights, channel_scales, own_peaks, all_peaks,
+    hidden_hbm, peaks_ref,
+    hidden_buf, rows_buf, weights, early_gates, channel_scales, own_peaks, all_peaks,
     send_sem, recv_sem, sib_send, sib_recv, peak_send, peak_recv, load_sem,
 ):
     me = lax.axis_index("tp")
@@ -44,6 +44,7 @@
     edges = [(tiles * s) // PIECES * LANES for s in range(PIECES + 1)]
     piece = [pl.ds(a, b - a) for a, b in zip(edges[:-1], edges[1:])]
     signs = (1, -1)
+    every = pl.ds(0, width)
 
     barrier = pltpu.get_barrier_semaphore()
     for device in (at(1), at(-1), sibling):
@@ -88,20 +89,30 @@
     nearer = 2 * (lax.rem(chip, group_chips) // (group_chips // 2)) - 1
     ranked = [lax.rem(first + groups + step, groups) for step in (0, nearer, -nearer, 2)]
 
-    def project(picked):
-        spans = [pl.ds(pl.multiple_of(ranked[i] * LANES, LANES), LANES) for i in picked]
-        x = jnp.concatenate([rows_buf[span, pl.ds(0, width)] for span in spans], axis=0)
-        values = lax.dot_general(
-            weights[...], x, (((1,), (1,)), ((), ())), preferred_element_type=jnp.float32
-        )
-        for i, span in enumerate(spans):
+    def spans_of(picked):
+        return [pl.ds(pl.multiple_of(ranked[i] * LANES, LANES), LANES) for i in picked]
+
+    def out_copy(i):
+        span = spans_of((i,))[0]
+        return pltpu.make_async_copy(hidden_buf.at[:, span], hidden_hbm.at[:, span], load_sem.at[3 + i])
+
+    def multiply(picked, part, depth):
+        x = jnp.concatenate([rows_buf[span, depth] for span in spans_of(picked)], axis=0)
+        return lax.dot_general(
+            weights[pl.ds(part * units, units), depth], x, (((1,), (1,)), ((), ())),
+            preferred_element_type=jnp.float32,
+        )
+
+    def finish(picked, gates, ups):
+        for i, span in enumerate(spans_of(picked)):
             spread = jnp.where(equal_ids(LANES, LANES), rows_buf[span, pl.ds(width, LANES)].astype(jnp.float32), 0.0)
             scale = jnp.sum(spread, axis=0, keepdims=True)
-            part = values[:, i * LANES:(i + 1) * LANES]
-            gate = part[:units] * scale * channel_scales[:, 0:1]
-            up = part[units:] * scale * channel_scales[:, 1:2]
+            lanes = slice(i * LANES, (i + 1) * LANES)
+            gate = gates[:, lanes] * scale * channel_scales[:, 0:1]
+            up = ups[:, lanes] * scale * channel_scales[:, 1:2]
             hidden = (gate / (1.0 + jnp.exp(-gate)) * up).astype(jnp.bfloat16)
-            hidden_ref[:, span] = hidden
+            hidden_buf[:, span] = hidden
+            out_copy(picked[i]).start()
             peak = jnp.max(jnp.abs(hidden.astype(jnp.float32)), axis=0, keepdims=True)
             own_peaks[pl.ds(ranked[picked[i]], 1), :] = peak
 
@@ -128,17 +139,21 @@
                 share(way, hop, s, block).start()
         if hop == 1:
             for k, ref in enumerate((gate_scales_ref, up_scales_ref)):
-                spread = jnp.where(equal_ids(units, units), ref[...], 0.0)
+                spread = jnp.where(equal_ids(units, units), ref[...].reshape(1, units), 0.0)
                 channel_scales[:, k:k + 1] = jnp.sum(spread, axis=1, keepdims=True)
         elif hop == 6:
             gate_copy.wait()
             up_copy.wait()
             for earlier in range(6):
                 wait_shared(earlier)
-            project((0, 1))
-    for earlier in (6, 7, 8):
-        wait_shared(earlier)
-    project((2, 3))
+            early_gates[...] = multiply((0, 1), 0, every)
+        elif hop == 7:
+            finish((0, 1), early_gates[...], multiply((0, 1), 1, every))
+            wait_shared(6)
+            wait_shared(7)
+            finish((2,), multiply((2,), 0, every), multiply((2,), 1, every))
+    wait_shared(8)
+    finish((3,), multiply((3,), 0, every), multiply((3,), 1, every))
 
     def peak_copy(step):
         return pltpu.make_async_remote_copy(
@@ -161,10 +176,20 @@
                     share(way, hop, s, me).wait_send()
     for s in range(PIECES):
         share(0, 0, s, me).wait_send()
+    for i in range(groups):
+        out_copy(i).wait()
     for step in reversed(order):
         peak_copy(step).wait()
     peaks = jnp.maximum(jnp.max(all_peaks[...], axis=0), own_peaks[...])
     peaks_ref[...] = jnp.maximum(peaks, 1e-5)
+
+
+def normalise(hidden_ref, peaks_ref, down_ref, row_peak_ref):
+    for g in range(peaks_ref.shape[0]):
+        span = slice(g * LANES, (g + 1) * LANES)
+        peak = peaks_ref[g:g + 1, :]
+        down_ref[:, span] = (hidden_ref[:, span].astype(jnp.float32) / peak).astype(jnp.bfloat16)
+        row_peak_ref[span] = peak.reshape(LANES)
 
 
 def shards(token_codes, token_scales, live_counts, gate_codes, up_codes, gate_scales, up_scales):
@@ -184,10 +209,12 @@
             jax.ShapeDtypeStruct((groups, LANES), jnp.float32),
         ),
         in_specs=[hbm, whole, pl.BlockSpec(memory_space=pltpu.SMEM), hbm, hbm, whole, whole],
-        out_specs=(whole, whole),
+        out_specs=(hbm, whole),
         scratch_shapes=[
+            pltpu.VMEM((units, row_count), jnp.bfloat16),
             pltpu.VMEM((row_count, width + LANES), jnp.bfloat16),
             pltpu.VMEM((2 * units, width), jnp.bfloat16),
+            pltpu.VMEM((units, 2 * LANES), jnp.float32),
             pltpu.VMEM((units, LANES), jnp.float32),
             pltpu.VMEM((groups, LANES), jnp.float32),
             pltpu.VMEM((tp - 1, groups, LANES), jnp.float32),
@@ -197,17 +224,24 @@
             dma((2, far + 1, PIECES)),
             dma((tp - 1,)),
             dma((tp - 1,)),
-            dma((3,)),
+            dma((3 + groups,)),
         ],
         compiler_params=pltpu.CompilerParams(
             collective_id=0, has_side_effects=True, vmem_limit_bytes=60 << 20
         ),
     )(
         token_codes, token_scales[None, :], live_counts, gate_codes.T, up_codes.T,
-        gate_scales[None, :], up_scales[None, :],
+        gate_scales, up_scales,
     )
-    row_peak = peaks.reshape(row_count)
-    down_input = (hidden.astype(jnp.float32) / row_peak[None, :]).astype(jnp.bfloat16)
+    down_input, row_peak = pl.pallas_call(
+        normalise,
+        out_shape=(
+            jax.ShapeDtypeStruct((units, row_count), jnp.bfloat16),
+            jax.ShapeDtypeStruct((row_count,), jnp.float32),
+        ),
+        in_specs=[whole, whole],
+        out_specs=(whole, whole),
+    )(hidden, peaks)
     return (down_input.T, row_peak)
 
 

time: 61.4 us -> 56.3 us (0.917)
  local copies, waits for them, and re-layouts: 3.75 us -> 0 us
  other arithmetic: 1.73 us -> 0 us
    broadcast_in_dim x2 -> x0, local copies, waits for them, and re-layouts: 2.49 us -> none  [the longest x1 1.25 us: shards(): gate_scales[None, :]]
    pallas_call x0 -> x1, Pallas kernels: none -> 1.75 us  [shards(): pl.pallas_call(normalise, out_shape=(jax.ShapeDtypeStruct((units, row_cou...]
    transpose x1 -> x0, other arithmetic: 1.73 us -> none  [shards(): return (down_input.T, row_peak)]
    pallas_call x1, Pallas kernels: 54.4 us -> 53.1 us  [shards(): pl.pallas_call(functools.partial(kernel, tp, width, units), out_shape=(ja...]
    unnamed x1 -> x0, local copies, waits for them, and re-layouts: 1.26 us -> none
where the time goes in v3:
time: 56.3 us; the launch traced here: 56.1 us
  Pallas kernels  54.8 us (97%)
  between operations  1.28 us (2%)
    pallas_call x1, Pallas kernels, shards(): pl.pallas_call(functools.partial(kernel, tp, width, units), out_shape=(ja...  53.1 us
    pallas_call x1, Pallas kernels, shards(): pl.pallas_call(normalise, out_shape=(jax.ShapeDtypeStruct((units, row_cou...  1.75 us

profile of v3, /device:TPU:1, one launch (start us, length us, event | category | flops | bytes accessed | tf_op | source)
XLA Modules:
  0.0 56.1 jit_solution(16456401113702235669)
XLA Ops:
  1.3 53.1 %shard_map.86 = (bf16[288,512]{1,0:T(8,128)(2,1)}, f32[4,128]{1,0:T(4,128)}) custom-call(bf16[16,3584]{1,0:T(8,128)(2,1)} %codes_hbm.1, bf16[1,16]{1,0:T(2,128)(2,1)} %bitcast.6, s32[1]{0:T(128)S(6)} %copy.9.counts_ref, bf16[288,3584]{1,0:T(8,128)(2,1)} %bitcast.4, bf16[288,3584]{1,0:T(8,128)(2,1)} %bitcast.5, f32[288]{0:T(512)} %gate_scales_ref.1, ...), custom_call_target="tpu_custom_call" | custom-call | tf_op jit(solution)/shard_map/pallas_call | solution.py:205
  54.3 1.7 %shard_map.87 = (bf16[288,512]{1,0:T(8,128)(2,1)}, f32[512]{0:T(512)}) custom-call(bf16[288,512]{1,0:T(8,128)(2,1)} %get-tuple-element.6.hidden_ref, f32[4,128]{1,0:T(4,128)} %get-tuple-element.7.peaks_ref), custom_call_target="tpu_custom_call" | custom-call | tf_op jit(solution)/shard_map/pallas_call | solution.py:236

commit v4 on v3

--- a/solution.py
+++ b/solution.py
@@ -9,8 +9,9 @@
 
 MESH = pl.DeviceIdType.MESH
 SLOTS = 16
-PIECES = 4
+PIECES = 6
 LANES = 128
+EXTRA = 2 * LANES
 
 
 def equal_ids(rows, columns):
@@ -28,28 +29,34 @@
     me = lax.axis_index("tp")
     chips = tp // 2
     far = chips // 2
-    sibling = me + 1 - 2 * lax.rem(me, 2)
+    core = lax.rem(me, 2)
+    sibling = me + 1 - 2 * core
     chip = me // 2
     groups = tp * SLOTS // LANES
     group_chips = chips // groups
-    full = width + LANES
-
-    def at(distance):
-        return lax.rem(me + 2 * distance + 2 * tp, tp)
+    full = width + EXTRA
+    every = pl.ds(0, width)
+
+    toward = 1 - 2 * core
+    ahead = lax.rem(me + 2 * toward + tp, tp)
+    behind = lax.rem(me - 2 * toward + tp, tp)
+    across = lax.rem(sibling - 2 * toward + tp, tp)
 
     def rows_of(device):
         return pl.ds(pl.multiple_of(device * SLOTS, SLOTS), SLOTS)
 
-    tiles = full // LANES
-    edges = [(tiles * s) // PIECES * LANES for s in range(PIECES + 1)]
-    piece = [pl.ds(a, b - a) for a, b in zip(edges[:-1], edges[1:])]
-    signs = (1, -1)
-    every = pl.ds(0, width)
+    def block(hop):
+        start = lax.rem(chip - toward * hop + chips, chips) * (2 * SLOTS)
+        return pl.ds(pl.multiple_of(start, 2 * SLOTS), 2 * SLOTS)
+
+    def piece(s, server):
+        index = lax.rem(s + server * (PIECES // 2), PIECES)
+        return pl.ds(pl.multiple_of(index * (full // PIECES), LANES), full // PIECES)
 
     barrier = pltpu.get_barrier_semaphore()
-    for device in (at(1), at(-1), sibling):
+    for device in (behind, across, sibling):
         pl.semaphore_signal(barrier, inc=1, device_id={"tp": device}, device_id_type=MESH)
-    own_copy = pltpu.make_async_copy(codes_hbm, rows_buf.at[rows_of(me), pl.ds(0, width)], load_sem.at[0])
+    own_copy = pltpu.make_async_copy(codes_hbm, rows_buf.at[rows_of(me), every], load_sem.at[0])
     own_copy.start()
     gate_copy = pltpu.make_async_copy(gate_hbm, weights.at[pl.ds(0, units)], load_sem.at[1])
     gate_copy.start()
@@ -58,32 +65,39 @@
     kept = equal_ids(SLOTS, SLOTS) & (lax.broadcasted_iota(jnp.int32, (SLOTS, SLOTS), 0) < counts_ref[0])
     spread = jnp.where(kept, scales_ref[...].astype(jnp.float32), 0.0)
     scale_col = jnp.sum(spread, axis=1, keepdims=True)
-    rows_buf[rows_of(me), pl.ds(width, LANES)] = jnp.broadcast_to(scale_col, (SLOTS, LANES)).astype(jnp.bfloat16)
+    rows_buf[rows_of(me), pl.ds(width, EXTRA)] = jnp.broadcast_to(scale_col, (SLOTS, EXTRA)).astype(jnp.bfloat16)
     own_copy.wait()
     pl.semaphore_wait(barrier, 3)
 
-    def active(way, hop, s):
-        return hop < far or (s < PIECES // 2) == (way == 0)
-
-    def ring(way, hop, s, block):
+    def remote(span, columns, send, recv, device):
+        part = rows_buf.at[span, columns]
         return pltpu.make_async_remote_copy(
-            src_ref=rows_buf.at[rows_of(block), piece[s]],
-            dst_ref=rows_buf.at[rows_of(block), piece[s]],
-            send_sem=send_sem.at[way, hop - 1, s],
-            recv_sem=recv_sem.at[way, hop - 1, s],
-            device_id={"tp": at(signs[way])},
-            device_id_type=MESH,
+            src_ref=part, dst_ref=part, send_sem=send, recv_sem=recv,
+            device_id={"tp": device}, device_id_type=MESH,
         )
 
-    def share(way, hop, s, block):
-        return pltpu.make_async_remote_copy(
-            src_ref=rows_buf.at[rows_of(block), piece[s]],
-            dst_ref=rows_buf.at[rows_of(block), piece[s]],
-            send_sem=sib_send.at[way, hop, s],
-            recv_sem=sib_recv.at[way, hop, s],
-            device_id={"tp": sibling},
-            device_id_type=MESH,
-        )
+    def ring(hop, s):
+        return remote(block(hop - 1), piece(s, core), send_sem.at[hop, s], recv_sem.at[hop, s], ahead)
+
+    def own(way, s):
+        server = core if way == 0 else 1 - core
+        device = ahead if way == 0 else across
+        return remote(rows_of(me), piece(s, server), send_sem.at[way, s], recv_sem.at[way, s], device)
+
+    def share(hop, s):
+        return remote(block(hop), piece(s, core), sib_send.at[hop, s], sib_recv.at[hop, s], sibling)
+
+    own_share = remote(rows_of(me), pl.ds(0, full), sib_send.at[0, 0], sib_recv.at[0, 0], sibling)
+
+    def pieces_at(hop):
+        return PIECES if hop < far else PIECES // 2
+
+    def wait_shared(hop):
+        if hop == 0:
+            own_share.wait_recv()
+        else:
+            for s in range(pieces_at(hop)):
+                share(hop, s).wait_recv()
 
     first = chip // group_chips
     nearer = 2 * (lax.rem(chip, group_chips) // (group_chips // 2)) - 1
@@ -116,27 +130,20 @@
             peak = jnp.max(jnp.abs(hidden.astype(jnp.float32)), axis=0, keepdims=True)
             own_peaks[pl.ds(ranked[picked[i]], 1), :] = peak
 
-    def wait_shared(hop):
-        for s in range(PIECES):
-            for way in (0, 1):
-                if active(way, hop, s) and not (hop == 0 and way == 1):
-                    share(way, hop, s, me).wait_recv()
-
     for s in range(PIECES):
-        for way in (0, 1):
-            ring(way, 1, s, me).start()
-    for s in range(PIECES):
-        share(0, 0, s, me).start()
+        own(0, s).start()
+        own(1, s).start()
+    own_share.start()
     for hop in range(1, far + 1):
-        for s in range(PIECES):
-            for way in (0, 1):
-                if not active(way, hop, s):
-                    continue
-                block = at(-signs[way] * hop)
-                ring(way, hop, s, block).wait_recv()
-                if hop < far and active(way, hop + 1, s):
-                    ring(way, hop + 1, s, block).start()
-                share(way, hop, s, block).start()
+        for s in range(pieces_at(hop)):
+            if hop == 1:
+                own(0, s).wait_recv()
+                own(1, s).wait_recv()
+            else:
+                ring(hop, s).wait_recv()
+            if hop < far and s < pieces_at(hop + 1):
+                ring(hop + 1, s).start()
+            share(hop, s).start()
         if hop == 1:
             for k, ref in enumerate((gate_scales_ref, up_scales_ref)):
                 spread = jnp.where(equal_ids(units, units), ref[...].reshape(1, units), 0.0)
@@ -168,14 +175,15 @@
     order = sorted(range(1, tp), key=lambda step: -min(step, tp - step))
     for step in order:
         peak_copy(step).start()
+    own_share.wait_send()
     for hop in range(1, far + 1):
-        for s in range(PIECES):
-            for way in (0, 1):
-                if active(way, hop, s):
-                    ring(way, hop, s, me).wait_send()
-                    share(way, hop, s, me).wait_send()
-    for s in range(PIECES):
-        share(0, 0, s, me).wait_send()
+        for s in range(pieces_at(hop)):
+            if hop == 1:
+                own(0, s).wait_send()
+                own(1, s).wait_send()
+            else:
+                ring(hop, s).wait_send()
+            share(hop, s).wait_send()
     for i in range(groups):
         out_copy(i).wait()
     for step in reversed(order):
@@ -212,16 +220,16 @@
         out_specs=(hbm, whole),
         scratch_shapes=[
             pltpu.VMEM((units, row_count), jnp.bfloat16),
-            pltpu.VMEM((row_count, width + LANES), jnp.bfloat16),
+            pltpu.VMEM((row_count, width + EXTRA), jnp.bfloat16),
             pltpu.VMEM((2 * units, width), jnp.bfloat16),
             pltpu.VMEM((units, 2 * LANES), jnp.float32),
             pltpu.VMEM((units, LANES), jnp.float32),
             pltpu.VMEM((groups, LANES), jnp.float32),
             pltpu.VMEM((tp - 1, groups, LANES), jnp.float32),
-            dma((2, far, PIECES)),
-            dma((2, far, PIECES)),
-            dma((2, far + 1, PIECES)),
-            dma((2, far + 1, PIECES)),
+            dma((far + 1, PIECES)),
+            dma((far + 1, PIECES)),
+            dma((far + 1, PIECES)),
+            dma((far + 1, PIECES)),
             dma((tp - 1,)),
             dma((tp - 1,)),
             dma((3 + groups,)),

time: 56.3 us -> 54 us (0.959)
  Pallas kernels: 54.8 us -> 52.5 us
    pallas_call x1, Pallas kernels: 53.1 us -> 50.8 us  [shards(): pl.pallas_call(functools.partial(kernel, tp, width, units), out_shape=(ja...]
where the time goes in v4:
time: 54 us; the launch traced here: 53.8 us
  Pallas kernels  52.5 us (97%)
  between operations  1.28 us (2%)
    pallas_call x1, Pallas kernels, shards(): pl.pallas_call(functools.partial(kernel, tp, width, units), out_shape=(ja...  50.8 us
    pallas_call x1, Pallas kernels, shards(): pl.pallas_call(normalise, out_shape=(jax.ShapeDtypeStruct((units, row_cou...  1.75 us

profile of v4, /device:TPU:1, one launch (start us, length us, event | category | flops | bytes accessed | tf_op | source)
XLA Modules:
  0.0 53.8 jit_solution(7373054511376921501)
XLA Ops:
  1.3 50.8 %shard_map.86 = (bf16[288,512]{1,0:T(8,128)(2,1)}, f32[4,128]{1,0:T(4,128)}) custom-call(bf16[16,3584]{1,0:T(8,128)(2,1)} %codes_hbm.1, bf16[1,16]{1,0:T(2,128)(2,1)} %bitcast.6, s32[1]{0:T(128)S(6)} %copy.9.counts_ref, bf16[288,3584]{1,0:T(8,128)(2,1)} %bitcast.4, bf16[288,3584]{1,0:T(8,128)(2,1)} %bitcast.5, f32[288]{0:T(512)} %gate_scales_ref.1, ...), custom_call_target="tpu_custom_call" | custom-call | tf_op jit(solution)/shard_map/pallas_call | solution.py:213
  52.0 1.7 %shard_map.87 = (bf16[288,512]{1,0:T(8,128)(2,1)}, f32[512]{0:T(512)}) custom-call(bf16[288,512]{1,0:T(8,128)(2,1)} %get-tuple-element.6.hidden_ref, f32[4,128]{1,0:T(4,128)} %get-tuple-element.7.peaks_ref), custom_call_target="tpu_custom_call" | custom-call | tf_op jit(solution)/shard_map/pallas_call | solution.py:244

commit v5 on v4

--- a/solution.py
+++ b/solution.py
@@ -21,9 +21,10 @@
 
 def kernel(
     tp, width, units,
-    codes_hbm, scales_ref, counts_ref, gate_hbm, up_hbm, gate_scales_ref, up_scales_ref,
+    codes_hbm, scales_hbm, counts_hbm, gate_hbm, up_hbm, gate_scales_hbm, up_scales_hbm,
     hidden_hbm, peaks_ref,
     hidden_buf, rows_buf, weights, early_gates, channel_scales, own_peaks, all_peaks,
+    scales_ref, counts_ref, gate_scales_ref, up_scales_ref,
     send_sem, recv_sem, sib_send, sib_recv, peak_send, peak_recv, load_sem,
 ):
     me = lax.axis_index("tp")
@@ -58,10 +59,21 @@
         pl.semaphore_signal(barrier, inc=1, device_id={"tp": device}, device_id_type=MESH)
     own_copy = pltpu.make_async_copy(codes_hbm, rows_buf.at[rows_of(me), every], load_sem.at[0])
     own_copy.start()
+    small_copies = [
+        pltpu.make_async_copy(source, target, load_sem.at[3 + groups + i])
+        for i, (source, target) in enumerate((
+            (scales_hbm, scales_ref), (counts_hbm, counts_ref),
+            (gate_scales_hbm, gate_scales_ref), (up_scales_hbm, up_scales_ref),
+        ))
+    ]
+    for copy in small_copies:
+        copy.start()
     gate_copy = pltpu.make_async_copy(gate_hbm, weights.at[pl.ds(0, units)], load_sem.at[1])
     gate_copy.start()
     up_copy = pltpu.make_async_copy(up_hbm, weights.at[pl.ds(units, units)], load_sem.at[2])
     up_copy.start()
+    small_copies[0].wait()
+    small_copies[1].wait()
     kept = equal_ids(SLOTS, SLOTS) & (lax.broadcasted_iota(jnp.int32, (SLOTS, SLOTS), 0) < counts_ref[0])
     spread = jnp.where(kept, scales_ref[...].astype(jnp.float32), 0.0)
     scale_col = jnp.sum(spread, axis=1, keepdims=True)
@@ -85,7 +97,11 @@
         return remote(rows_of(me), piece(s, server), send_sem.at[way, s], recv_sem.at[way, s], device)
 
     def share(hop, s):
-        return remote(block(hop), piece(s, core), sib_send.at[hop, s], sib_recv.at[hop, s], sibling)
+        columns = pl.ds(0, full) if hop < far else piece(s, core)
+        return remote(block(hop), columns, sib_send.at[hop, s], sib_recv.at[hop, s], sibling)
+
+    def shares_at(hop):
+        return 1 if hop < far else PIECES // 2
 
     own_share = remote(rows_of(me), pl.ds(0, full), sib_send.at[0, 0], sib_recv.at[0, 0], sibling)
 
@@ -96,7 +112,7 @@
         if hop == 0:
             own_share.wait_recv()
         else:
-            for s in range(pieces_at(hop)):
+            for s in range(shares_at(hop)):
                 share(hop, s).wait_recv()
 
     first = chip // group_chips
@@ -143,8 +159,11 @@
                 ring(hop, s).wait_recv()
             if hop < far and s < pieces_at(hop + 1):
                 ring(hop + 1, s).start()
-            share(hop, s).start()
+            if hop == far or s == PIECES - 1:
+                share(hop, 0 if hop < far else s).start()
         if hop == 1:
+            small_copies[2].wait()
+            small_copies[3].wait()
             for k, ref in enumerate((gate_scales_ref, up_scales_ref)):
                 spread = jnp.where(equal_ids(units, units), ref[...].reshape(1, units), 0.0)
                 channel_scales[:, k:k + 1] = jnp.sum(spread, axis=1, keepdims=True)
@@ -156,11 +175,9 @@
             early_gates[...] = multiply((0, 1), 0, every)
         elif hop == 7:
             finish((0, 1), early_gates[...], multiply((0, 1), 1, every))
-            wait_shared(6)
-            wait_shared(7)
-            finish((2,), multiply((2,), 0, every), multiply((2,), 1, every))
-    wait_shared(8)
-    finish((3,), multiply((3,), 0, every), multiply((3,), 1, every))
+    for earlier in (6, 7, 8):
+        wait_shared(earlier)
+    finish((2, 3), multiply((2, 3), 0, every), multiply((2, 3), 1, every))
 
     def peak_copy(step):
         return pltpu.make_async_remote_copy(
@@ -183,6 +200,7 @@
                 own(1, s).wait_send()
             else:
                 ring(hop, s).wait_send()
+        for s in range(shares_at(hop)):
             share(hop, s).wait_send()
     for i in range(groups):
         out_copy(i).wait()
@@ -216,7 +234,7 @@
             jax.ShapeDtypeStruct((units, row_count), jnp.bfloat16),
             jax.ShapeDtypeStruct((groups, LANES), jnp.float32),
         ),
-        in_specs=[hbm, whole, pl.BlockSpec(memory_space=pltpu.SMEM), hbm, hbm, whole, whole],
+        in_specs=[hbm] * 7,
         out_specs=(hbm, whole),
         scratch_shapes=[
             pltpu.VMEM((units, row_count), jnp.bfloat16),
@@ -226,13 +244,17 @@
             pltpu.VMEM((units, LANES), jnp.float32),
             pltpu.VMEM((groups, LANES), jnp.float32),
             pltpu.VMEM((tp - 1, groups, LANES), jnp.float32),
+            pltpu.VMEM((1, SLOTS), jnp.bfloat16),
+            pltpu.SMEM((1,), jnp.int32),
+            pltpu.VMEM((units,), jnp.float32),
+            pltpu.VMEM((units,), jnp.float32),
             dma((far + 1, PIECES)),
             dma((far + 1, PIECES)),
             dma((far + 1, PIECES)),
             dma((far + 1, PIECES)),
             dma((tp - 1,)),
             dma((tp - 1,)),
-            dma((3 + groups,)),
+            dma((7 + groups,)),
         ],
         compiler_params=pltpu.CompilerParams(
             collective_id=0, has_side_effects=True, vmem_limit_bytes=60 << 20

time: 54 us -> 52.3 us (0.969)
  Pallas kernels: 52.5 us -> 50.9 us
    pallas_call x1, Pallas kernels: 50.8 us -> 49.1 us  [shards(): pl.pallas_call(functools.partial(kernel, tp, width, units), out_shape=(ja...]
where the time goes in v5:
time: 52.3 us; the launch traced here: 52.2 us
  Pallas kernels  50.9 us (97%)
  between operations  1.28 us (2%)
    pallas_call x1, Pallas kernels, shards(): pl.pallas_call(functools.partial(kernel, tp, width, units), out_shape=(ja...  49.1 us
    pallas_call x1, Pallas kernels, shards(): pl.pallas_call(normalise, out_shape=(jax.ShapeDtypeStruct((units, row_cou...  1.75 us

profile of v5, /device:TPU:1, one launch (start us, length us, event | category | flops | bytes accessed | tf_op | source)
XLA Modules:
  0.0 52.2 jit_solution(14963041571980584721)
XLA Ops:
  1.3 49.1 %shard_map.86 = (bf16[288,512]{1,0:T(8,128)(2,1)}, f32[4,128]{1,0:T(4,128)}) custom-call(bf16[16,3584]{1,0:T(8,128)(2,1)} %codes_hbm.1, bf16[1,16]{1,0:T(2,128)(2,1)} %bitcast.6, s32[1]{0:T(128)S(6)} %copy.9.counts_hbm, bf16[288,3584]{1,0:T(8,128)(2,1)} %bitcast.4, bf16[288,3584]{1,0:T(8,128)(2,1)} %bitcast.5, f32[288]{0:T(512)} %gate_scales_hbm.1, ...), custom_call_target="tpu_custom_call" | custom-call | tf_op jit(solution)/shard_map/pallas_call | solution.py:231
  50.4 1.7 %shard_map.87 = (bf16[288,512]{1,0:T(8,128)(2,1)}, f32[512]{0:T(512)}) custom-call(bf16[288,512]{1,0:T(8,128)(2,1)} %get-tuple-element.6.hidden_ref, f32[4,128]{1,0:T(4,128)} %get-tuple-element.7.peaks_ref), custom_call_target="tpu_custom_call" | custom-call | tf_op jit(solution)/shard_map/pallas_call | solution.py:266

commit v6 on v5

--- a/solution.py
+++ b/solution.py
@@ -23,9 +23,9 @@
     tp, width, units,
     codes_hbm, scales_hbm, counts_hbm, gate_hbm, up_hbm, gate_scales_hbm, up_scales_hbm,
     hidden_hbm, peaks_ref,
-    hidden_buf, rows_buf, weights, early_gates, channel_scales, own_peaks, all_peaks,
+    hidden_buf, rows_buf, weights, early_gates, channel_scales, own_peaks, all_peaks, sibling_peaks,
     scales_ref, counts_ref, gate_scales_ref, up_scales_ref,
-    send_sem, recv_sem, sib_send, sib_recv, peak_send, peak_recv, load_sem,
+    send_sem, recv_sem, sib_send, sib_recv, peak_send, peak_recv, early_send, early_recv, load_sem,
 ):
     me = lax.axis_index("tp")
     chips = tp // 2
@@ -78,6 +78,8 @@
     spread = jnp.where(kept, scales_ref[...].astype(jnp.float32), 0.0)
     scale_col = jnp.sum(spread, axis=1, keepdims=True)
     rows_buf[rows_of(me), pl.ds(width, EXTRA)] = jnp.broadcast_to(scale_col, (SLOTS, EXTRA)).astype(jnp.bfloat16)
+    own_peaks[...] = jnp.zeros_like(own_peaks)
+    all_peaks[...] = jnp.zeros_like(all_peaks)
     own_copy.wait()
     pl.semaphore_wait(barrier, 3)
 
@@ -118,6 +120,9 @@
     first = chip // group_chips
     nearer = 2 * (lax.rem(chip, group_chips) // (group_chips // 2)) - 1
     ranked = [lax.rem(first + groups + step, groups) for step in (0, nearer, -nearer, 2)]
+
+    low = lax.rem(first + 1 + (nearer + 1) // 2, groups)
+    late_pair, early_pair = pl.ds(low, 2), pl.ds(low + 2, 2)
 
     def spans_of(picked):
         return [pl.ds(pl.multiple_of(ranked[i] * LANES, LANES), LANES) for i in picked]
@@ -144,7 +149,12 @@
             hidden_buf[:, span] = hidden
             out_copy(picked[i]).start()
             peak = jnp.max(jnp.abs(hidden.astype(jnp.float32)), axis=0, keepdims=True)
-            own_peaks[pl.ds(ranked[picked[i]], 1), :] = peak
+            own_peaks[low + lax.rem(ranked[picked[i]] - low + groups, groups), :, :] = peak
+
+    swap = pltpu.make_async_remote_copy(
+        src_ref=own_peaks.at[early_pair], dst_ref=sibling_peaks, send_sem=early_send.at[0], recv_sem=early_recv.at[0],
+        device_id={"tp": sibling}, device_id_type=MESH,
+    )
 
     for s in range(PIECES):
         own(0, s).start()
@@ -175,23 +185,36 @@
             early_gates[...] = multiply((0, 1), 0, every)
         elif hop == 7:
             finish((0, 1), early_gates[...], multiply((0, 1), 1, every))
-    for earlier in (6, 7, 8):
-        wait_shared(earlier)
-    finish((2, 3), multiply((2, 3), 0, every), multiply((2, 3), 1, every))
-
-    def peak_copy(step):
+            swap.start()
+
+    def peak_copy(step, pair, send, recv):
         return pltpu.make_async_remote_copy(
-            src_ref=own_peaks,
-            dst_ref=all_peaks.at[step - 1],
-            send_sem=peak_send.at[step - 1],
-            recv_sem=peak_recv.at[step - 1],
+            src_ref=own_peaks.at[pair],
+            dst_ref=all_peaks.at[step - 1, pair],
+            send_sem=send.at[step - 1],
+            recv_sem=recv.at[step - 1],
             device_id={"tp": lax.rem(me + step, tp)},
             device_id_type=MESH,
         )
 
+    def early(step):
+        return peak_copy(step, early_pair, early_send, early_recv)
+
+    def late(step):
+        return peak_copy(step, late_pair, peak_send, peak_recv)
+
     order = sorted(range(1, tp), key=lambda step: -min(step, tp - step))
+    wait_shared(6)
+    wait_shared(7)
+    swap.wait()
+    own_peaks[early_pair, :, :] = jnp.maximum(own_peaks[early_pair, :, :], sibling_peaks[...])
     for step in order:
-        peak_copy(step).start()
+        if step % 2 == 0:
+            early(step).start()
+    wait_shared(8)
+    finish((2, 3), multiply((2, 3), 0, every), multiply((2, 3), 1, every))
+    for step in order:
+        late(step).start()
     own_share.wait_send()
     for hop in range(1, far + 1):
         for s in range(pieces_at(hop)):
@@ -205,9 +228,12 @@
     for i in range(groups):
         out_copy(i).wait()
     for step in reversed(order):
-        peak_copy(step).wait()
+        if step % 2 == 0:
+            early(step).wait()
+        late(step).wait()
     peaks = jnp.maximum(jnp.max(all_peaks[...], axis=0), own_peaks[...])
-    peaks_ref[...] = jnp.maximum(peaks, 1e-5)
+    for g in range(groups):
+        peaks_ref[g:g + 1, :] = jnp.maximum(jnp.maximum(peaks[g], peaks[g + groups]), 1e-5)
 
 
 def normalise(hidden_ref, peaks_ref, down_ref, row_peak_ref):
@@ -242,8 +268,9 @@
             pltpu.VMEM((2 * units, width), jnp.bfloat16),
             pltpu.VMEM((units, 2 * LANES), jnp.float32),
             pltpu.VMEM((units, LANES), jnp.float32),
-            pltpu.VMEM((groups, LANES), jnp.float32),
-            pltpu.VMEM((tp - 1, groups, LANES), jnp.float32),
+            pltpu.VMEM((2 * groups, 1, LANES), jnp.float32),
+            pltpu.VMEM((tp - 1, 2 * groups, 1, LANES), jnp.float32),
+            pltpu.VMEM((2, 1, LANES), jnp.float32),
             pltpu.VMEM((1, SLOTS), jnp.bfloat16),
             pltpu.SMEM((1,), jnp.int32),
             pltpu.VMEM((units,), jnp.float32),
@@ -252,6 +279,8 @@
             dma((far + 1, PIECES)),
             dma((far + 1, PIECES)),
             dma((far + 1, PIECES)),
+            dma((tp - 1,)),
+            dma((tp - 1,)),
             dma((tp - 1,)),
             dma((tp - 1,)),
             dma((7 + groups,)),

time: 52.3 us -> 52.2 us (level)
  no operation moved by 1% of the time
where the time goes in v6:
time: 52.2 us; the launch traced here: 52.1 us
  Pallas kernels  50.8 us (97%)
  between operations  1.28 us (2%)
    pallas_call x1, Pallas kernels, shards(): pl.pallas_call(functools.partial(kernel, tp, width, units), out_shape=(ja...  49.1 us
    pallas_call x1, Pallas kernels, shards(): pl.pallas_call(normalise, out_shape=(jax.ShapeDtypeStruct((units, row_cou...  1.75 us

profile of v6, /device:TPU:1, one launch (start us, length us, event | category | flops | bytes accessed | tf_op | source)
XLA Modules:
  0.0 52.1 jit_solution(3990751337171960827)
XLA Ops:
  1.3 49.1 %shard_map.86 = (bf16[288,512]{1,0:T(8,128)(2,1)}, f32[4,128]{1,0:T(4,128)}) custom-call(bf16[16,3584]{1,0:T(8,128)(2,1)} %codes_hbm.1, bf16[1,16]{1,0:T(2,128)(2,1)} %bitcast.6, s32[1]{0:T(128)S(6)} %copy.9.counts_hbm, bf16[288,3584]{1,0:T(8,128)(2,1)} %bitcast.4, bf16[288,3584]{1,0:T(8,128)(2,1)} %bitcast.5, f32[288]{0:T(512)} %gate_scales_hbm.1, ...), custom_call_target="tpu_custom_call" | custom-call | tf_op jit(solution)/shard_map/pallas_call | solution.py:257
  50.4 1.7 %shard_map.87 = (bf16[288,512]{1,0:T(8,128)(2,1)}, f32[512]{0:T(512)}) custom-call(bf16[288,512]{1,0:T(8,128)(2,1)} %get-tuple-element.6.hidden_ref, f32[4,128]{1,0:T(4,128)} %get-tuple-element.7.peaks_ref), custom_call_target="tpu_custom_call" | custom-call | tf_op jit(solution)/shard_map/pallas_call | solution.py:295

commit v7 on v6

--- a/solution.py
+++ b/solution.py
@@ -156,6 +156,23 @@
         device_id={"tp": sibling}, device_id_type=MESH,
     )
 
+    def peak_copy(step, pair, send, recv):
+        return pltpu.make_async_remote_copy(
+            src_ref=own_peaks.at[pair],
+            dst_ref=all_peaks.at[step - 1, pair],
+            send_sem=send.at[step - 1],
+            recv_sem=recv.at[step - 1],
+            device_id={"tp": lax.rem(me + step, tp)},
+            device_id_type=MESH,
+        )
+
+    def early(step):
+        return peak_copy(step, early_pair, early_send, early_recv)
+
+    def late(step):
+        return peak_copy(step, late_pair, peak_send, peak_recv)
+
+    order = sorted(range(1, tp), key=lambda step: -min(step, tp - step))
     for s in range(PIECES):
         own(0, s).start()
         own(1, s).start()
@@ -182,34 +199,19 @@
             up_copy.wait()
             for earlier in range(6):
                 wait_shared(earlier)
-            early_gates[...] = multiply((0, 1), 0, every)
+            finish((0, 1), multiply((0, 1), 0, every), multiply((0, 1), 1, every))
+            swap.start()
         elif hop == 7:
-            finish((0, 1), early_gates[...], multiply((0, 1), 1, every))
-            swap.start()
-
-    def peak_copy(step, pair, send, recv):
-        return pltpu.make_async_remote_copy(
-            src_ref=own_peaks.at[pair],
-            dst_ref=all_peaks.at[step - 1, pair],
-            send_sem=send.at[step - 1],
-            recv_sem=recv.at[step - 1],
-            device_id={"tp": lax.rem(me + step, tp)},
-            device_id_type=MESH,
-        )
-
-    def early(step):
-        return peak_copy(step, early_pair, early_send, early_recv)
-
-    def late(step):
-        return peak_copy(step, late_pair, peak_send, peak_recv)
-
-    order = sorted(range(1, tp), key=lambda step: -min(step, tp - step))
-    wait_shared(6)
+            swap.wait()
+            own_peaks[early_pair, :, :] = jnp.maximum(own_peaks[early_pair, :, :], sibling_peaks[...])
+            wait_shared(6)
+            for step in order:
+                if step % 2 == 0 and min(step, tp - step) // 2 <= 6:
+                    early(step).start()
+
     wait_shared(7)
-    swap.wait()
-    own_peaks[early_pair, :, :] = jnp.maximum(own_peaks[early_pair, :, :], sibling_peaks[...])
     for step in order:
-        if step % 2 == 0:
+        if step % 2 == 0 and min(step, tp - step) // 2 > 6:
             early(step).start()
     wait_shared(8)
     finish((2, 3), multiply((2, 3), 0, every), multiply((2, 3), 1, every))

time: 52.2 us -> 52.2 us (level)
  no operation moved by 1% of the time
where the time goes in v7:
time: 52.2 us; the launch traced here: 52.1 us
  Pallas kernels  50.8 us (97%)
  between operations  1.28 us (2%)
    pallas_call x1, Pallas kernels, shards(): pl.pallas_call(functools.partial(kernel, tp, width, units), out_shape=(ja...  49 us
    pallas_call x1, Pallas kernels, shards(): pl.pallas_call(normalise, out_shape=(jax.ShapeDtypeStruct((units, row_cou...  1.75 us

profile of v7, /device:TPU:1, one launch (start us, length us, event | category | flops | bytes accessed | tf_op | source)
XLA Modules:
  0.0 52.1 jit_solution(17155114513151053325)
XLA Ops:
  1.3 49.0 %shard_map.86 = (bf16[288,512]{1,0:T(8,128)(2,1)}, f32[4,128]{1,0:T(4,128)}) custom-call(bf16[16,3584]{1,0:T(8,128)(2,1)} %codes_hbm.1, bf16[1,16]{1,0:T(2,128)(2,1)} %bitcast.6, s32[1]{0:T(128)S(6)} %copy.9.counts_hbm, bf16[288,3584]{1,0:T(8,128)(2,1)} %bitcast.4, bf16[288,3584]{1,0:T(8,128)(2,1)} %bitcast.5, f32[288]{0:T(512)} %gate_scales_hbm.1, ...), custom_call_target="tpu_custom_call" | custom-call | tf_op jit(solution)/shard_map/pallas_call | solution.py:259
  50.3 1.7 %shard_map.87 = (bf16[288,512]{1,0:T(8,128)(2,1)}, f32[512]{0:T(512)}) custom-call(bf16[288,512]{1,0:T(8,128)(2,1)} %get-tuple-element.6.hidden_ref, f32[4,128]{1,0:T(4,128)} %get-tuple-element.7.peaks_ref), custom_call_target="tpu_custom_call" | custom-call | tf_op jit(solution)/shard_map/pallas_call | solution.py:297

commit v8 on v6

--- a/solution.py
+++ b/solution.py
@@ -23,7 +23,7 @@
     tp, width, units,
     codes_hbm, scales_hbm, counts_hbm, gate_hbm, up_hbm, gate_scales_hbm, up_scales_hbm,
     hidden_hbm, peaks_ref,
-    hidden_buf, rows_buf, weights, early_gates, channel_scales, own_peaks, all_peaks, sibling_peaks,
+    hidden_buf, rows_buf, weights, channel_scales, own_peaks, all_peaks, sibling_peaks,
     scales_ref, counts_ref, gate_scales_ref, up_scales_ref,
     send_sem, recv_sem, sib_send, sib_recv, peak_send, peak_recv, early_send, early_recv, load_sem,
 ):
@@ -177,14 +177,12 @@
             for k, ref in enumerate((gate_scales_ref, up_scales_ref)):
                 spread = jnp.where(equal_ids(units, units), ref[...].reshape(1, units), 0.0)
                 channel_scales[:, k:k + 1] = jnp.sum(spread, axis=1, keepdims=True)
-        elif hop == 6:
+        elif hop == 7:
             gate_copy.wait()
             up_copy.wait()
             for earlier in range(6):
                 wait_shared(earlier)
-            early_gates[...] = multiply((0, 1), 0, every)
-        elif hop == 7:
-            finish((0, 1), early_gates[...], multiply((0, 1), 1, every))
+            finish((0, 1), multiply((0, 1), 0, every), multiply((0, 1), 1, every))
             swap.start()
 
     def peak_copy(step, pair, send, recv):
@@ -266,7 +264,6 @@
             pltpu.VMEM((units, row_count), jnp.bfloat16),
             pltpu.VMEM((row_count, width + EXTRA), jnp.bfloat16),
             pltpu.VMEM((2 * units, width), jnp.bfloat16),
-            pltpu.VMEM((units, 2 * LANES), jnp.float32),
             pltpu.VMEM((units, LANES), jnp.float32),
             pltpu.VMEM((2 * groups, 1, LANES), jnp.float32),
             pltpu.VMEM((tp - 1, 2 * groups, 1, LANES), jnp.float32),

time: 52.2 us -> 52.3 us (level)
  no operation moved by 1% of the time
where the time goes in v8:
time: 52.3 us; the launch traced here: 52.1 us
  Pallas kernels  50.8 us (97%)
  between operations  1.28 us (2%)
    pallas_call x1, Pallas kernels, shards(): pl.pallas_call(functools.partial(kernel, tp, width, units), out_shape=(ja...  49.1 us
    pallas_call x1, Pallas kernels, shards(): pl.pallas_call(normalise, out_shape=(jax.ShapeDtypeStruct((units, row_cou...  1.75 us

profile of v8, /device:TPU:1, one launch (start us, length us, event | category | flops | bytes accessed | tf_op | source)
XLA Modules:
  0.0 52.1 jit_solution(11767189461554892756)
XLA Ops:
  1.3 49.1 %shard_map.86 = (bf16[288,512]{1,0:T(8,128)(2,1)}, f32[4,128]{1,0:T(4,128)}) custom-call(bf16[16,3584]{1,0:T(8,128)(2,1)} %codes_hbm.1, bf16[1,16]{1,0:T(2,128)(2,1)} %bitcast.6, s32[1]{0:T(128)S(6)} %copy.9.counts_hbm, bf16[288,3584]{1,0:T(8,128)(2,1)} %bitcast.4, bf16[288,3584]{1,0:T(8,128)(2,1)} %bitcast.5, f32[288]{0:T(512)} %gate_scales_hbm.1, ...), custom_call_target="tpu_custom_call" | custom-call | tf_op jit(solution)/shard_map/pallas_call | solution.py:255
  50.4 1.7 %shard_map.87 = (bf16[288,512]{1,0:T(8,128)(2,1)}, f32[512]{0:T(512)}) custom-call(bf16[288,512]{1,0:T(8,128)(2,1)} %get-tuple-element.6.hidden_ref, f32[4,128]{1,0:T(4,128)} %get-tuple-element.7.peaks_ref), custom_call_target="tpu_custom_call" | custom-call | tf_op jit(solution)/shard_map/pallas_call | solution.py:292
